TPU v7x, 512 devices: a whole 4x4x16 slice. The times are simulated.
512 devices in a mesh: dp: 8 (over x, core), expert: 64 (over y, z).
Axes of the slice: x: 4, y: 4, z: 16, core: 2. Of those that a mesh axis runs over, the one named last changes fastest.
Arguments:
- tokens: bfloat16 [8192, 4096], P('expert', 'dp'), may hold values from -6 to 6
- slot_of: int32 [8192, 8], P('expert'), may hold values from 0 to 95, as said below
- weight_of: float32 [8192, 8], P('expert'), may hold values from 0.05 to 0.5
- gate_up: bfloat16 [64, 2, 4096, 1024], P('expert', None, 'dp')
- down_proj: bfloat16 [64, 1024, 4096], P('expert', None, 'dp')
- spare_up: bfloat16 [64, 2, 4096, 512], P('expert', None, 'dp'), as said below
- spare_down: bfloat16 [64, 1024, 2048], P('expert', None, 'dp'), as said below
Outputs:
- mixed: bfloat16 [8192, 4096], P('expert', 'dp')
Inputs may be any that keep to these rules, and one draw needn't show every extreme that they name: `slot_of`: slot e < 64 is expert e's own slot; slot 64 + r is a replica of one of two hot experts, each hot expert having half of the replicas; the 8 entries of a row serve distinct experts. In every aligned block of 128 rows (the rows of one index of expert) no slot serves more than 16 entries and some slot exactly 16, and no expert (own slot and replicas together) is served more than 64 times, some exactly 64 times. spare_up[2 r + h] equals gate_up[e] restricted to hidden units h * 512 to (h + 1) * 512 - 1, for the expert e that slot 64 + r replicates. spare_down[2 r + h] holds the columns of down_proj[e] that the first step assigns to half h, for the expert e that slot 64 + r replicates.
All inputs are finite; a program needn't handle non-finite values.
Results may differ from a plain program's by a relative error of at most 0.029.
Values may be sent and summed in bfloat16 or wider, within the bound.
A program may use at most 128 MiB of HBM per device.

v0:
```python
import jax
import jax.numpy as jnp
from jax import lax
from jax.sharding import PartitionSpec as P


def partner_2(value, axis, stride):
    mask = 2**stride
    pairs = [(source, source ^ mask) for source in range(lax.axis_size(axis))]
    return lax.ppermute(value, axis, pairs)


def silu_product(summed):
    return (jax.nn.silu(summed[:, :, 0, :]) * summed[:, :, 1, :]).astype(jnp.bfloat16)


def on_device(tokens, slot_of, weight_of, gate_up, down_proj, spare_up, spare_down):
    row_count, feat_width = tokens.shape
    top_count = slot_of.shape[1]
    ff_width = gate_up.shape[3]
    half_ff = ff_width // 2
    half_feat = feat_width // 2
    expert_count = lax.axis_size("expert")
    my_index = lax.axis_index("expert")
    parity = my_index % 2
    assign_count = row_count * top_count
    flat_slot = slot_of.reshape(assign_count)
    own_depth = 7 * row_count // (expert_count - 8)
    place_count = expert_count + expert_count // 2
    own_span = 2 * own_depth
    slot_table = (flat_slot[:, None] == jnp.arange(place_count, dtype=jnp.int32)[None, :]).astype(
        jnp.int32
    )
    earlier = jnp.cumsum(slot_table, axis=0) - slot_table
    slot_rank = jnp.sum(earlier * slot_table, axis=1)
    positions = flat_slot * own_depth + slot_rank
    source_index = jnp.full((place_count * own_depth,), assign_count, jnp.int32)
    source_index = source_index.at[positions].set(jnp.arange(assign_count, dtype=jnp.int32))
    source_table = source_index.reshape(place_count, own_depth)
    partner_rows = source_table[expert_count + jnp.arange(expert_count, dtype=jnp.int32) // 2]
    dest_table = jnp.concatenate([source_table[:expert_count], partner_rows], 1)
    row_pick = jnp.where(dest_table < assign_count, dest_table // top_count, row_count)
    padded = jnp.concatenate([tokens, jnp.zeros((1, feat_width), tokens.dtype)], 0)
    outgoing = padded[row_pick]
    arrived = lax.all_to_all(outgoing, "expert", split_axis=0, concat_axis=0, tiled=True)
    up_blocks = gate_up[0].reshape(2, feat_width, 2, half_ff)
    partials = jnp.einsum(
        "ecd,qdhf->echqf", arrived[:, :own_depth], up_blocks, preferred_element_type=jnp.float32
    )
    partials = partials.reshape(expert_count, own_span, 2, half_ff)
    spare_part = jnp.einsum(
        "ecd,qdf->ecqf", arrived[:, own_depth:], spare_up[0], preferred_element_type=jnp.float32
    )
    partials = jnp.concatenate([partials, spare_part], 1)
    hidden = silu_product(lax.psum(partials.astype(jnp.bfloat16), "dp").astype(jnp.float32))
    partner = partner_2(hidden[:, own_span:], "expert", 0)
    down_own = down_proj[0].reshape(2, half_ff, feat_width)
    own_hidden = hidden[:, :own_span].reshape(expert_count, own_depth, 2, half_ff)
    own_out = jnp.einsum("echf,hfd->ecd", own_hidden, down_own, preferred_element_type=jnp.float32)
    pieces = [own_out.reshape(expert_count, own_span, half_feat)]
    mine = hidden[:, own_span:]
    whole_hidden = jnp.where(
        parity == 0, jnp.concatenate([mine, partner], 2), jnp.concatenate([partner, mine], 2)
    )
    pieces.append(
        jnp.einsum("ecf,fd->ecd", whole_hidden, spare_down[0], preferred_element_type=jnp.float32)
    )
    expert_out = jnp.concatenate(pieces, 1).astype(jnp.bfloat16)
    returned = lax.all_to_all(expert_out, "expert", split_axis=0, concat_axis=0, tiled=True)
    answer_table = returned[:, :own_span].reshape(expert_count * own_depth, feat_width)
    spare_back = returned[:, own_span:].reshape(expert_count // 2, 2, own_depth, half_feat)
    spare_back = spare_back.transpose(0, 2, 1, 3).reshape(expert_count // 2 * own_depth, feat_width)
    answer_table = jnp.concatenate([answer_table, spare_back], 0)
    answers = answer_table[positions].reshape(row_count, top_count, feat_width)
    mixed = jnp.sum(weight_of[:, :, None] * answers.astype(jnp.float32), axis=1)
    return mixed.astype(jnp.bfloat16)


def solution(mesh):
    in_specs = (
        P("expert", "dp"),
        P("expert", None),
        P("expert", None),
        P("expert", None, "dp", None),
        P("expert", None, "dp"),
        P("expert", None, "dp", None),
        P("expert", None, "dp"),
    )
    out_specs = P("expert", "dp")
    return jax.shard_map(
        on_device, mesh=mesh, in_specs=in_specs, out_specs=out_specs, check_vma=False
    )
```

profile of v0, /device:TPU:6, one launch (start us, length us, event | category | flops | bytes accessed | tf_op | source)
XLA Modules:
  0.0 421.8 jit_solution(3146700205094278341)
XLA Ops:
  6.5 0.8 broadcast_multiply_fusion
  7.3 0.8 copy.14
  8.5 27.0 %reduce-window.6 = s32[96,8,128]{2,1,0:T(8,128)S(1)} reduce-window(s32[96,8,128]{2,1,0:T(8,128)S(1)} %fusion.19, s32[]{:T(128)} %constant.60.clone.1), window={size=1x1x128 pad=0_0x0_0x127_0}, to_apply=%region_0.1 | reduce-window | flops 12484608 | bytes 786436 | tf_op jit(solution)/shard_map/reduce-window
  36.3 4.3 %scatter_custom_fusion = s32[1536]{0:T(1024)S(1)} fusion(s32[1024]{0:T(1024)S(1)} %bitcast.89, s32[1024]{0:T(1024)S(1)} %iota.15, s32[]{:T(128)} %constant.58.clone.1), kind=kCustom, calls=%fused_computation.49 | custom fusion | bytes 6148 | tf_op jit(solution)/shard_map/scatter | solution.py:38
  40.9 0.6 gather_fusion
  41.7 9.2 %gather_fusion.1 = bf16[2048,512]{1,0:T(8,128)(2,1)} fusion(bf16[129,512]{1,0:T(8,128)(2,1)S(1)} %concatenate.58, s32[2048]{0:T(1024)S(1)} %broadcast_clamp_fusion), kind=kCustom, calls=%fused_computation.1 | custom fusion | bytes 4202496 | tf_op jit(solution)/shard_map/gather | solution.py:44
  50.8 19.1 %all-to-all-start = ((bf16[64,32,512]{2,1,0:T(8,128)(2,1)}), bf16[64,32,512]{2,1,0:T(8,128)(2,1)}, u32[]{:S(2)}, u32[]{:S(2)}) async-start(bf16[64,32,512]{2,1,0:T(8,128)(2,1)} %bitcast.6), calls=%async_computation | async-start | bytes 4194304 | tf_op jit(solution)/shard_map/all_to_all | solution.py:45
  70.2 2.8 reshape_squeeze.6
  73.0 94.1 %all-to-all-done = bf16[64,32,512]{2,1,0:T(8,128)(2,1)} async-done(((bf16[64,32,512]{2,1,0:T(8,128)(2,1)}), bf16[64,32,512]{2,1,0:T(8,128)(2,1)}, u32[]{:S(2)}, u32[]{:S(2)}) %all-to-all-start) | async-done | bytes 2097184 | tf_op jit(solution)/shard_map/all_to_all | solution.py:45
  167.1 2.5 convolution_convert_fusion
  169.6 1.2 copy.20
  170.7 0.4 copy-done.3
  171.1 3.6 convert_bitcast_fusion
  174.7 2.4 copy.19
  177.1 3.2 pad_maximum_fusion
  180.3 91.9 %all-reduce.3.cloned.1.call-done = bf16[64,48,2,512]{3,0,2,1:T(8,128)(2,1)} async-done(((bf16[64,48,2,512]{3,0,2,1:T(8,128)(2,1)}), bf16[64,48,2,512]{3,0,2,1:T(8,128)(2,1)}) %all-reduce.3.cloned.1.call-update) | async-done | bytes 6291472 | tf_op jit(solution)/shard_map/psum | solution.py:55
  272.3 4.6 %convert_element_type.26 = f32[64,48,2,512]{3,0,2,1:T(8,128)S(1)} convert(bf16[64,48,2,512]{3,0,2,1:T(8,128)(2,1)} %all-reduce.3.cloned.1.call-done) | non-fusion elementwise | flops 3145728 | bytes 18874368 | tf_op jit(solution)/shard_map/convert_element_type | solution.py:55
  276.9 2.2 fusion.1
  279.2 1.1 slice.68
  280.3 3.7 collective-permute-start
  284.2 1.0 copy-done.6
  285.2 1.3 bitcast_convert_fusion
  286.5 0.4 reshape.315
  286.9 21.4 %collective-permute-done = bf16[64,16,512]{2,0,1:T(8,128)(2,1)} collective-permute-done((bf16[64,16,512]{2,0,1:T(8,128)(2,1)}, bf16[64,16,512]{2,0,1:T(8,128)(2,1)}, u32[]{:S(2)}, u32[]{:S(2)}) %collective-permute-start) | collective-permute-done | bytes 1048608 | tf_op jit(solution)/shard_map/ppermute | solution.py:10
  308.4 3.1 maximum_select_fusion
  311.5 1.3 fusion.11
  312.8 1.3 pad_maximum_fusion.1
  314.1 15.8 %all-to-all-start.1 = ((bf16[64,48,256]{2,1,0:T(8,128)(2,1)}), bf16[64,48,256]{2,1,0:T(8,128)(2,1)S(1)}, u32[]{:S(2)}, u32[]{:S(2)}) async-start(bf16[64,48,256]{2,1,0:T(8,128)(2,1)} %pad_maximum_fusion.1), calls=%async_computation.1 | async-start | bytes 3145728 | tf_op jit(solution)/shard_map/all_to_all | solution.py:69
  330.0 76.0 %all-to-all-done.1 = bf16[64,48,256]{2,1,0:T(8,128)(2,1)S(1)} async-done(((bf16[64,48,256]{2,1,0:T(8,128)(2,1)}), bf16[64,48,256]{2,1,0:T(8,128)(2,1)S(1)}, u32[]{:S(2)}, u32[]{:S(2)}) %all-to-all-start.1) | async-done | bytes 1572896 | tf_op jit(solution)/shard_map/all_to_all | solution.py:69
  406.1 0.5 copy.24
  407.3 5.1 %gather_fusion.2 = bf16[1024,512]{1,0:T(8,128)(2,1)} fusion(bf16[1536,512]{1,0:T(8,128)(2,1)S(1)} %pad_maximum_fusion.2, s32[1024]{0:T(1024)S(1)} %broadcast_clamp_fusion.1), kind=kCustom, calls=%fused_computation.2 | custom fusion | bytes 2101248 | tf_op jit(solution)/shard_map/gather | solution.py:74
  412.4 2.6 fusion.2
  (47 shorter events, 2.9 us)
Async XLA Ops:
  6.5 160.5 %copy-start = (bf16[1,2,512,512]{3,2,1,0:T(8,128)(2,1)S(1)}, bf16[1,2,512,512]{3,2,1,0:T(8,128)(2,1)}, u32[]{:S(2)}) copy-start(bf16[1,2,512,512]{3,2,1,0:T(8,128)(2,1)} %param.12) | copy-start | bytes 3145732
  8.5 33.1 %copy-start.4 = (bf16[128,512]{1,0:T(8,128)(2,1)S(1)}, bf16[128,512]{1,0:T(8,128)(2,1)}, u32[]{:S(2)}) copy-start(bf16[128,512]{1,0:T(8,128)(2,1)} %param.7) | copy-start | bytes 393220
  50.8 19.4 %copy-start.2 = (bf16[1,2,512,1024]{3,2,1,0:T(8,128)(2,1)S(1)}, bf16[1,2,512,1024]{3,2,1,0:T(8,128)(2,1)}, u32[]{:S(2)}) copy-start(bf16[1,2,512,1024]{3,2,1,0:T(8,128)(2,1)} %param.10) | copy-start | bytes 6291460
  50.8 116.2 %all-to-all-start = ((bf16[64,32,512]{2,1,0:T(8,128)(2,1)}), bf16[64,32,512]{2,1,0:T(8,128)(2,1)}, u32[]{:S(2)}, u32[]{:S(2)}) async-start(bf16[64,32,512]{2,1,0:T(8,128)(2,1)} %bitcast.6), calls=%async_computation | async-start | bytes 4194304 | tf_op jit(solution)/shard_map/all_to_all | solution.py:45
  70.0 202.3 %all-reduce.3.cloned.1.call-start = ((), (), s32[]{:S(2)}) async-start(), calls=%async_computation.2 | async-start | bytes 12582912 | tf_op jit(solution)/shard_map/psum | solution.py:55
  169.5 1.6 copy-start.3
  280.3 28.1 %collective-permute-start = (bf16[64,16,512]{2,0,1:T(8,128)(2,1)}, bf16[64,16,512]{2,0,1:T(8,128)(2,1)}, u32[]{:S(2)}, u32[]{:S(2)}) collective-permute-start(bf16[64,16,512]{2,0,1:T(8,128)(2,1)} %slice.68), channel_id=1, source_target_pairs={{0,1},{1,0},{2,3},{3,2},{4,5},{5,4},{6,7},{7,6},{8,9},{9,8},{10,11... | collective-permute-start | bytes 3145736 | tf_op jit(solution)/shard_map/ppermute | solution.py:10
  283.9 1.2 copy-start.6
  286.9 24.6 %copy-start.7 = (bf16[1,1024,256]{2,1,0:T(8,128)(2,1)S(1)}, bf16[1,1024,256]{2,1,0:T(8,128)(2,1)}, u32[]{:S(2)}) copy-start(bf16[1,1024,256]{2,1,0:T(8,128)(2,1)} %param.13) | copy-start | bytes 1572868
  314.1 15.8 %copy-start.5 = (f32[128,8]{0,1:T(8,128)S(1)}, f32[128,8]{0,1:T(8,128)}, u32[]{:S(2)}) copy-start(f32[128,8]{0,1:T(8,128)} %param.9) | copy-start | bytes 12292
  314.1 91.9 %all-to-all-start.1 = ((bf16[64,48,256]{2,1,0:T(8,128)(2,1)}), bf16[64,48,256]{2,1,0:T(8,128)(2,1)S(1)}, u32[]{:S(2)}, u32[]{:S(2)}) async-start(bf16[64,48,256]{2,1,0:T(8,128)(2,1)} %pad_maximum_fusion.1), calls=%async_computation.1 | async-start | bytes 3145728 | tf_op jit(solution)/shard_map/all_to_all | solution.py:69
  407.3 7.7 %copy-start.1 = (bf16[1,2,512,512]{3,2,1,0:T(8,128)(2,1)S(1)}, bf16[1,2,512,512]{3,2,1,0:T(8,128)(2,1)}, u32[]{:S(2)}) copy-start(bf16[1,2,512,512]{3,2,1,0:T(8,128)(2,1)} %param.12) | copy-start | bytes 3145732
Sparse Core Ops, SparseCore 0:
  180.5 91.7 all-reduce.2
where the time goes:
time: 422 us
  waiting for transfers between devices  283 us (67%)
  other arithmetic  45.4 us (11%)
  starting transfers between devices  38.8 us (9%)
  local copies, waits for them, and re-layouts  31.7 us (8%)
  between operations  13.7 us (3%)
  matrix products  8.69 us (2%)
    all_to_all x1, waiting for transfers between devices, on_device(): lax.all_to_all(outgoing, 'expert', split_axis=0, concat_axis=0, tiled=True)  94.1 us
    psum x1, waiting for transfers between devices, on_device(): lax.psum(partials.astype(jnp.bfloat16), 'dp').astype(jnp.float32)  91.9 us
    all_to_all x1, waiting for transfers between devices, on_device(): lax.all_to_all(expert_out, 'expert', split_axis=0, concat_axis=0, tiled=T...  76 us
    another operation x3, other arithmetic  27.2 us
    ppermute x1, waiting for transfers between devices, partner_2(): return lax.ppermute(value, axis, pairs)  21.4 us
    all_to_all x1, starting transfers between devices, on_device(): lax.all_to_all(outgoing, 'expert', split_axis=0, concat_axis=0, tiled=True)  19.1 us
    all_to_all x1, starting transfers between devices, on_device(): lax.all_to_all(expert_out, 'expert', split_axis=0, concat_axis=0, tiled=T...  15.8 us
    gather x1, local copies, waits for them, and re-layouts, on_device(): outgoing = padded[row_pick]  9.16 us
  transfers between devices with their start and end apart: 4, of which 4 were waited for; matrix products, arithmetic and copies ran while one was open for 1% of the time, Pallas kernels for 0%

commit v1 on v0

v1 whole, which is shorter than its diff:
```python
import jax
import jax.numpy as jnp
from jax import lax
from jax.experimental import pallas as pl
from jax.experimental.pallas import tpu as pltpu
from jax.sharding import PartitionSpec as P

NX, NY, NZ = 4, 4, 16
CAP = 16
BF = jnp.bfloat16
F32 = jnp.float32
MESH = pl.DeviceIdType.MESH
UNITS = NZ // 2
STAGE0 = 4
STEPS = UNITS + STAGE0 + 9


def mod(value, n):
    return lax.rem(value, n)


def kernel(
    tok_ref, meta_ref, gate_ref, down_ref, sup_ref, sdown_ref, out_ref,
    wall, wd, wsd, tok_all, meta_all, sel, arr, part, crecv, qbuf, rhalf, rfull, hid, outs,
    rland, oland, back, dense, zsend, zland,
    w_sem, z_s, z_r, m_s, m_r, y_s, y_r, yr_s, yr_r, c_s, c_r, xa_s, xa_r, xb_s, xb_r, p_s, p_r,
    g_s, g_r, h_s, h_r, ch_s, ch_r, o_s, o_r, or_s, or_r, zz_s, zz_r,
):
    dp = lax.axis_index("dp")
    ex = lax.axis_index("expert")
    x, c = dp // 2, mod(dp, 2)
    y, z = ex // NZ, mod(ex, NZ)
    half = mod(z, 2)
    pair = z // 2
    x1, x2, x3 = mod(x + 1, NX), mod(x + 2, NX), mod(x + 3, NX)
    y1, y2, y3 = mod(y + 1, NY), mod(y + 2, NY), mod(y + 3, NY)
    z1, z3 = mod(z + 1, NZ), mod(z + NZ - 1, NZ)
    dev_xp, dev_xm = (x1 * 2 + c, ex), (x3 * 2 + c, ex)
    dev_c = (x * 2 + (1 - c), ex)
    dev_yp, dev_ym = (dp, y1 * NZ + z), (dp, y3 * NZ + z)
    dev_zp, dev_zm = (dp, y * NZ + z1), (dp, y * NZ + z3)
    dev_pt = (dp, y * NZ + pair * 2 + (1 - half))

    def rc(src, dst, ssem, rsem, dev):
        return pltpu.make_async_remote_copy(
            src_ref=src, dst_ref=dst, send_sem=ssem, recv_sem=rsem, device_id=dev, device_id_type=MESH
        )

    loads = [
        pltpu.make_async_copy(gate_ref.at[0, 0], wall.at[:, 0:1024], w_sem.at[0]),
        pltpu.make_async_copy(gate_ref.at[0, 1], wall.at[:, 1024:2048], w_sem.at[1]),
        pltpu.make_async_copy(sup_ref.at[0, 0], wall.at[:, 2048:2560], w_sem.at[2]),
        pltpu.make_async_copy(sup_ref.at[0, 1], wall.at[:, 2560:3072], w_sem.at[3]),
        pltpu.make_async_copy(down_ref.at[0], wd, w_sem.at[4]),
        pltpu.make_async_copy(sdown_ref.at[0], wsd, w_sem.at[5]),
    ]
    for load in loads:
        load.start()

    tok_all[z] = tok_ref[...]
    meta_all[z] = meta_ref[...]

    barrier = pltpu.get_barrier_semaphore()
    for dev in (dev_xp, dev_xm, dev_c, dev_yp, dev_ym, dev_zp, dev_zm):
        pl.semaphore_signal(barrier, inc=1, device_id=dev, device_id_type=MESH)
    pl.semaphore_wait(barrier, 7)

    def z_block(d, i):
        return mod(z + NZ - i, NZ) if d == 0 else mod(z + i, NZ)

    def z_copy(d, i, k, block):
        piece = tok_all.at[block, 64 * k:64 * k + 64]
        return rc(piece, piece, z_s.at[d, i, k], z_r.at[d, i, k], dev_zp if d == 0 else dev_zm)

    def m_copy(d, i, block):
        piece = meta_all.at[block]
        return rc(piece, piece, m_s.at[d, i], m_r.at[d, i], dev_zp if d == 0 else dev_zm)

    def hop_send(d, i, k):
        z_copy(d, i, k, z_block(d, i)).start()

    def hop_wait(d, i, k):
        z_copy(d, i, k, z_block(d, i + 1)).wait_recv()

    for d in (0, 1):
        m_copy(d, 0, z_block(d, 0)).start()
    for k in (0, 1):
        for d in (0, 1):
            hop_send(d, 0, k)

    group = lax.broadcasted_iota(jnp.int32, (8, 128), 0)
    tri = (
        lax.broadcasted_iota(jnp.int32, (128, 128), 0) < lax.broadcasted_iota(jnp.int32, (128, 128), 1)
    ).astype(BF)
    place = lax.broadcasted_iota(jnp.int32, (8, CAP, 128), 1).astype(F32)

    def slot_ids(row, spare):
        own = row * NZ + z
        return jnp.where(spare == 1, NY * NZ + own // 2, own).astype(F32)

    send_ids = slot_ids(mod(y + group // 2 + 1, NY), mod(group, 2))
    back_ids = slot_ids(mod(group, 4), group // 4)

    def codes(meta, ids):
        mask = jnp.zeros((8, 128), F32)
        for k in range(8):
            mask = mask + jnp.where(meta[k:k + 1, :] == ids, 1.0, 0.0)
        rank = jnp.dot(mask.astype(BF), tri, preferred_element_type=F32)
        code = jnp.where(mask > 0.5, rank, -1.0)
        return jnp.broadcast_to(code[:, None, :], (8, CAP, 128)) == place

    def y_copy(block, n):
        if n == 0:
            return rc(sel.at[block, 0:32], arr.at[block, y], y_s.at[block, 0], y_r.at[block, 0], dev_yp)
        if n == 1:
            return rc(sel.at[block, 64:96], arr.at[block, y], y_s.at[block, 1], y_r.at[block, 1], dev_ym)
        if n == 2:
            return rc(sel.at[block, 32:48], rland.at[block, 0], y_s.at[block, 2], y_r.at[block, 2], dev_yp)
        return rc(sel.at[block, 48:64], rland.at[block, 1], y_s.at[block, 3], y_r.at[block, 3], dev_ym)

    def yr_copy(block, n):
        if n == 0:
            return rc(rland.at[block, 0], arr.at[block, y3, 0:16], yr_s.at[block, 0], yr_r.at[block, 0], dev_yp)
        return rc(rland.at[block, 1], arr.at[block, y1, 16:32], yr_s.at[block, 1], yr_r.at[block, 1], dev_ym)

    def select(block):
        hot = codes(meta_all[block], send_ids)
        pick = jnp.where(hot, 1.0, 0.0).astype(BF).reshape(128, 128)
        rows = jnp.dot(pick, tok_all[block], preferred_element_type=F32).astype(BF)
        sel[block] = rows
        for n in (2, 3, 0, 1):
            y_copy(block, n).start()
        arr[block, y] = rows[96:128]

    def relay(block):
        y_copy(block, 2).wait_recv()
        yr_copy(block, 0).start()
        y_copy(block, 3).wait_recv()
        yr_copy(block, 1).start()

    def arrivals(block):
        y_copy(block, 0).wait_recv()
        y_copy(block, 1).wait_recv()
        yr_copy(block, 0).wait_recv()
        yr_copy(block, 1).wait_recv()

    def unit_of(u):
        sign = 2 * mod(u, 2) - 1
        return mod(pair + ((u + 1) // 2) * sign + UNITS, UNITS)

    def c_copy(u):
        return rc(part.at[u, 1 - c], crecv.at[u], c_s.at[u], c_r.at[u], dev_c)

    def xa_copy(u, n):
        if n == 0:
            return rc(qbuf.at[u, x2, :, 0:1536], rhalf.at[u, 0], xa_s.at[u, 0], xa_r.at[u, 0], dev_xp)
        return rc(qbuf.at[u, x2, :, 1536:3072], rhalf.at[u, 1], xa_s.at[u, 1], xa_r.at[u, 1], dev_xm)

    def xb_copy(u, n):
        if n == 0:
            return rc(qbuf.at[u, x1], rfull.at[u, 0], xb_s.at[u, 0], xb_r.at[u, 0], dev_xp)
        return rc(qbuf.at[u, x3], rfull.at[u, 1], xb_s.at[u, 1], xb_r.at[u, 1], dev_xm)

    def p_copy(u):
        piece = hid.at[u, c, x, :, pl.ds(pl.multiple_of(1024 + half * 512, 512), 512)]
        return rc(piece, piece, p_s.at[u], p_r.at[u], dev_pt)

    def g_copy(u, n):
        piece = hid.at[u, c, x]
        return rc(piece, piece, g_s.at[u, n], g_r.at[u, n], dev_xp if n == 0 else dev_xm)

    def h_copy(u, n):
        if n == 0:
            piece = hid.at[u, c, x3, :, 0:1024]
            return rc(piece, piece, h_s.at[u, 0], h_r.at[u, 0], dev_xp)
        piece = hid.at[u, c, x1, :, 1024:2048]
        return rc(piece, piece, h_s.at[u, 1], h_r.at[u, 1], dev_xm)

    def ch_copy(u):
        piece = hid.at[u, c]
        return rc(piece, piece, ch_s.at[u], ch_r.at[u], dev_c)

    def o_copy(u, n):
        if n == 0:
            return rc(outs.at[u, y1], back.at[u, y], o_s.at[u, 0], o_r.at[u, 0], dev_yp)
        if n == 1:
            return rc(outs.at[u, y3], back.at[u, y], o_s.at[u, 1], o_r.at[u, 1], dev_ym)
        if n == 2:
            return rc(
                outs.at[u, y2, :, :, 0:384], oland.at[u, 0], o_s.at[u, 2], o_r.at[u, 2], dev_yp
            )
        return rc(
            outs.at[u, y2, :, :, 384:768], oland.at[u, 1], o_s.at[u, 3], o_r.at[u, 3], dev_ym
        )

    def or_copy(u, n):
        if n == 0:
            return rc(
                oland.at[u, 0], back.at[u, y3, :, :, 0:384], or_s.at[u, 0], or_r.at[u, 0], dev_yp
            )
        return rc(
            oland.at[u, 1], back.at[u, y1, :, :, 384:768], or_s.at[u, 1], or_r.at[u, 1], dev_ym
        )

    def multiply_up(u):
        @pl.when(u == 0)
        def _():
            for load in loads[:4]:
                load.wait()

        q = unit_of(u)
        arrivals(2 * q)
        arrivals(2 * q + 1)
        own = arr[pl.ds(2 * q, 2), :, 0:16, :].reshape(128, 512)
        spare = arr[pl.ds(2 * q, 2), :, 16:32, :].reshape(128, 512)
        for n in range(6):
            cols = slice(512 * n, 512 * n + 512)
            made = jnp.dot(own if n < 4 else spare, wall[:, cols], preferred_element_type=F32)
            part[u, :, :, :, cols] = made.astype(BF).reshape(2, 4, 16, 512)
        c_copy(u).start()

    def add_core(u):
        c_copy(u).wait_recv()
        for n, row in enumerate((x2, x1, x3, x)):
            qbuf[u, row] = (part[u, c, row].astype(F32) + crecv[u, row].astype(F32)).astype(BF)
            if n == 0:
                xa_copy(u, 0).start()
                xa_copy(u, 1).start()

    def add_far(u):
        for n, row, cols in ((0, x1, slice(0, 1536)), (1, x3, slice(1536, 3072))):
            xa_copy(u, n).wait_recv()
            both = qbuf[u, row, :, cols].astype(F32) + rhalf[u, n].astype(F32)
            qbuf[u, row, :, cols] = both.astype(BF)
            xb_copy(u, n).start()

    def activate(u):
        xb_copy(u, 0).wait_recv()
        xb_copy(u, 1).wait_recv()

        def total(low, width):
            cols = slice(low, low + width)
            mine = qbuf[u, x, :, cols].astype(F32)
            return mine + rfull[u, 0, :, cols].astype(F32) + rfull[u, 1, :, cols].astype(F32)

        def silu_product(low, width):
            gate = total(low, width)
            return (gate / (1.0 + jnp.exp(-gate)) * total(low + width, width)).astype(BF)

        at = pl.ds(pl.multiple_of(1024 + half * 512, 512), 512)
        hid[u, c, x, :, at] = silu_product(2048, 512)
        p_copy(u).start()
        hid[u, c, x, :, 0:1024] = silu_product(0, 1024)

    def gather_near(u):
        p_copy(u).wait_recv()
        g_copy(u, 0).start()
        g_copy(u, 1).start()

    def gather_far(u):
        for n in (0, 1):
            g_copy(u, n).wait_recv()
            h_copy(u, n).start()

    def gather_core(u):
        h_copy(u, 0).wait_recv()
        h_copy(u, 1).wait_recv()
        ch_copy(u).start()

    def multiply_down(u):
        @pl.when(u == 0)
        def _():
            for load in loads[4:]:
                load.wait()

        ch_copy(u).wait_recv()
        own = hid[u, :, :, :, 0:1024].reshape(128, 1024)
        spare = hid[u, :, :, :, 1024:2048].reshape(128, 1024)
        own_out = jnp.dot(own, wd[...], preferred_element_type=F32).astype(BF).reshape(2, 4, 16, 512)
        spare_out = jnp.dot(spare, wsd[...], preferred_element_type=F32).astype(BF).reshape(2, 4, 16, 256)
        for p in (0, 1):
            outs[u, :, p, :, 0:512] = own_out[p]
            outs[u, :, p, :, 512:768] = spare_out[p]
        for n in (2, 3, 0, 1):
            o_copy(u, n).start()
        back[u, y] = outs[u, y]

    def relay_back(u):
        for n in (0, 1):
            o_copy(u, 2 + n).wait_recv()
            or_copy(u, n).start()

    def combine(u):
        for n in (0, 1):
            o_copy(u, n).wait_recv()
            or_copy(u, n).wait_recv()
        q = unit_of(u)
        at = pl.ds(pl.multiple_of(half * 256, 256), 256)
        for p in (0, 1):
            block = 2 * q + p
            meta = meta_all[block]
            share = jnp.zeros((8, 128), F32)
            for k in range(8):
                share = share + jnp.where(meta[k:k + 1, :] == back_ids, meta[8 + k:9 + k, :], 0.0)
            spread = jnp.broadcast_to(share[:, None, :], (8, CAP, 128))
            weight = jnp.where(codes(meta, back_ids), spread, 0.0).astype(BF).reshape(128, 128)
            own = back[u, :, p, :, 0:512].reshape(64, 512)
            spare = back[u, :, p, :, 512:768].reshape(64, 256)
            over = (((0,), (0,)), ((), ()))
            dense[block] = lax.dot_general(weight[0:64], own, over, preferred_element_type=F32)
            more = lax.dot_general(weight[64:128], spare, over, preferred_element_type=F32)
            dense[block, :, at] = dense[block, :, at] + more

    def hops(t):
        @pl.when((t >= 1) & (t <= 7))
        def _():
            for d in (0, 1):
                m_copy(d, t - 1, z_block(d, t)).wait_recv()
            m_copy(0, t, z_block(0, t)).start()

            @pl.when(t <= 6)
            def _():
                m_copy(1, t, z_block(1, t)).start()

            for k in (0, 1):
                for d in (0, 1):
                    hop_wait(d, t - 1, k)
                    if k == d:
                        hop_send(d, t, k)
                    else:
                        @pl.when(t <= 6)
                        def _():
                            hop_send(d, t, k)

        @pl.when(t == 8)
        def _():
            m_copy(0, 7, z_block(0, 8)).wait_recv()
            hop_wait(0, 7, 0)
            hop_wait(1, 7, 1)

    stages = [
        (4 + 9, combine), (4 + 8, relay_back), (4 + 6, gather_core), (4 + 5, gather_far),
        (4 + 4, gather_near), (4 + 3, activate), (4 + 2, add_far), (4 + 1, add_core),
        (4 + 7, multiply_down), (4, multiply_up),
    ]

    def step(t, carry):
        hops(t)

        @pl.when((t >= 1) & (t <= 9))
        def _():
            relay(z_block(0, t - 1))

        @pl.when((t >= 2) & (t <= 8))
        def _():
            relay(z_block(1, t - 1))

        for offset, stage in stages:
            @pl.when((t >= offset) & (t < offset + UNITS))
            def _():
                stage(t - offset)

        @pl.when(t <= 8)
        def _():
            select(z_block(0, t))

        @pl.when((t >= 1) & (t <= 7))
        def _():
            select(z_block(1, t))

        return carry

    lax.fori_loop(0, STEPS, step, 0)

    def zz_copy(d, j, k):
        rows = slice(64 * k, 64 * k + 64)
        return rc(
            zsend.at[d, j, rows], zland.at[d, j, rows], zz_s.at[d, j, k], zz_r.at[d, j, k],
            dev_zm if d == 0 else dev_zp,
        )

    def chain(j, first, second):
        for k in (0, 1):
            rows = slice(64 * k, 64 * k + 64)
            for d in (0, 1):
                if first and k != d:
                    continue
                block = mod(z + NZ - 8 + j, NZ) if d == 0 else mod(z + 8 - j, NZ)
                value = dense[block, rows]
                if not first and not (second and k != d):
                    zz_copy(d, j - 1, k).wait_recv()
                    value = value + zland[d, j - 1, rows].astype(F32)
                zsend[d, j, rows] = value.astype(BF)
                zz_copy(d, j, k).start()

    chain(0, True, False)
    chain(1, False, True)

    def chain_step(j, carry):
        chain(j, False, False)
        return carry

    lax.fori_loop(2, 8, chain_step, 0)
    for k in (0, 1):
        rows = slice(64 * k, 64 * k + 64)
        for d in (0, 1):
            zz_copy(d, 7, k).wait_recv()
        value = dense[z, rows] + zland[0, 7, rows].astype(F32) + zland[1, 7, rows].astype(F32)
        out_ref[rows] = value.astype(BF)

    def drain_hops(i, carry):
        m_copy(0, i, z_block(0, i)).wait_send()
        for d in (0, 1):
            z_copy(d, i, d, z_block(d, i)).wait_send()
            zz_copy(d, i, d).wait_send()

        @pl.when(i <= 6)
        def _():
            m_copy(1, i, z_block(1, i)).wait_send()
            for d in (0, 1):
                z_copy(d, i, 1 - d, z_block(d, i)).wait_send()
                zz_copy(d, i + 1, 1 - d).wait_send()

        return carry

    lax.fori_loop(0, 8, drain_hops, 0)

    def drain_blocks(block, carry):
        for n in range(4):
            y_copy(block, n).wait_send()
        for n in range(2):
            yr_copy(block, n).wait_send()
        return carry

    lax.fori_loop(0, NZ, drain_blocks, 0)

    def drain_units(u, carry):
        c_copy(u).wait_send()
        p_copy(u).wait_send()
        ch_copy(u).wait_send()
        for n in range(2):
            for copy in (xa_copy, xb_copy, g_copy, h_copy, or_copy):
                copy(u, n).wait_send()
        for n in range(4):
            o_copy(u, n).wait_send()
        return carry

    lax.fori_loop(0, UNITS, drain_units, 0)


def on_device(tokens, slot_of, weight_of, gate_up, down_proj, spare_up, spare_down):
    meta = jnp.concatenate([slot_of.T.astype(F32), weight_of.T], 0)
    vmem = pl.BlockSpec(memory_space=pltpu.VMEM)
    hbm = pl.BlockSpec(memory_space=pl.ANY)
    dma = pltpu.SemaphoreType.DMA
    return pl.pallas_call(
        kernel,
        out_shape=jax.ShapeDtypeStruct((128, 512), BF),
        in_specs=[vmem, vmem, hbm, hbm, hbm, hbm],
        out_specs=vmem,
        scratch_shapes=[
            pltpu.VMEM((512, 3072), BF),
            pltpu.VMEM((1024, 512), BF),
            pltpu.VMEM((1024, 256), BF),
            pltpu.VMEM((NZ, 128, 512), BF),
            pltpu.VMEM((NZ, 16, 128), F32),
            pltpu.VMEM((NZ, 128, 512), BF),
            pltpu.VMEM((NZ, NY, 32, 512), BF),
            pltpu.VMEM((UNITS, 2, 4, 16, 3072), BF),
            pltpu.VMEM((UNITS, 4, 16, 3072), BF),
            pltpu.VMEM((UNITS, 4, 16, 3072), BF),
            pltpu.VMEM((UNITS, 2, 16, 1536), BF),
            pltpu.VMEM((UNITS, 2, 16, 3072), BF),
            pltpu.VMEM((UNITS, 2, 4, 16, 2048), BF),
            pltpu.VMEM((UNITS, 4, 2, 16, 768), BF),
            pltpu.VMEM((NZ, 2, 16, 512), BF),
            pltpu.VMEM((UNITS, 2, 2, 16, 384), BF),
            pltpu.VMEM((UNITS, 4, 2, 16, 768), BF),
            pltpu.VMEM((NZ, 128, 512), F32),
            pltpu.VMEM((2, 8, 128, 512), BF),
            pltpu.VMEM((2, 8, 128, 512), BF),
            dma((6,)),
            dma((2, 8, 2)), dma((2, 8, 2)),
            dma((2, 8)), dma((2, 8)),
            dma((NZ, 4)), dma((NZ, 4)),
            dma((NZ, 2)), dma((NZ, 2)),
            dma((UNITS,)), dma((UNITS,)),
            dma((UNITS, 2)), dma((UNITS, 2)),
            dma((UNITS, 2)), dma((UNITS, 2)),
            dma((UNITS,)), dma((UNITS,)),
            dma((UNITS, 2)), dma((UNITS, 2)),
            dma((UNITS, 2)), dma((UNITS, 2)),
            dma((UNITS,)), dma((UNITS,)),
            dma((UNITS, 4)), dma((UNITS, 4)),
            dma((UNITS, 2)), dma((UNITS, 2)),
            dma((2, 8, 2)), dma((2, 8, 2)),
        ],
        compiler_params=pltpu.CompilerParams(
            collective_id=0, has_side_effects=True, vmem_limit_bytes=58 * 1024 * 1024
        ),
        cost_estimate=pl.CostEstimate(flops=5 * 10**9, bytes_accessed=6 * 10**6, transcendentals=10**5),
    )(tokens, meta, gate_up, down_proj, spare_up, spare_down)


def solution(mesh):
    in_specs = (
        P("expert", "dp"),
        P("expert", None),
        P("expert", None),
        P("expert", None, "dp", None),
        P("expert", None, "dp"),
        P("expert", None, "dp", None),
        P("expert", None, "dp"),
    )
    out_specs = P("expert", "dp")
    return jax.shard_map(
        on_device, mesh=mesh, in_specs=in_specs, out_specs=out_specs, check_vma=False
    )
```

time: 422 us -> 155 us (0.37)
  waiting for transfers between devices: 283 us -> 0 us
  Pallas kernels: 0 us -> 151 us
  other arithmetic: 45.4 us -> 1.97 us
  starting transfers between devices: 38.8 us -> 0 us
  local copies, waits for them, and re-layouts: 31.7 us -> 1.57 us
  between operations: 13.7 us -> 0.01 us
  matrix products: 8.69 us -> 0 us
    all_to_all x2 -> x0, waiting for transfers between devices: 170 us -> none  [the longest x1 94.1 us: on_device(): lax.all_to_all(outgoing, 'expert', split_axis=0, concat_axis=0, tiled=True)]
    pallas_call x0 -> x1, Pallas kernels: none -> 151 us  [on_device(): pl.pallas_call(kernel, out_shape=jax.ShapeDtypeStruct((128, 512), BF), in...]
    psum x1 -> x0, waiting for transfers between devices: 91.9 us -> none  [on_device(): lax.psum(partials.astype(jnp.bfloat16), 'dp').astype(jnp.float32)]
    all_to_all x2 -> x0, starting transfers between devices: 34.9 us -> none  [the longest x1 19.1 us: on_device(): lax.all_to_all(outgoing, 'expert', split_axis=0, concat_axis=0, tiled=True)]
    another operation x3 -> x0, other arithmetic: 27.2 us -> none
    ppermute x1 -> x0, waiting for transfers between devices: 21.4 us -> none  [partner_2(): return lax.ppermute(value, axis, pairs)]
    gather x3 -> x0, local copies, waits for them, and re-layouts: 14.8 us -> none  [the longest x1 9.16 us: on_device(): outgoing = padded[row_pick]]
    dot_general x4 -> x0, matrix products: 8.69 us -> none  [the longest x1 3.57 us: on_device(): jnp.einsum('ecd,qdhf->echqf', arrived[:, :own_depth], up_blocks, preferre...]
  transfers between devices with their start and end apart: 4 -> 0, of which waited for: 4 -> 0; matrix products, arithmetic and copies ran while one was open for 1% -> 0% of each run, Pallas kernels for 0% -> 0%
where the time goes in v1:
time: 155 us; the launch traced here: 154 us
  Pallas kernels  151 us (97%)
  other arithmetic  1.97 us (1%)
  local copies, waits for them, and re-layouts  1.57 us (1%)
    pallas_call x1, Pallas kernels, on_device(): pl.pallas_call(kernel, out_shape=jax.ShapeDtypeStruct((128, 512), BF), in...  151 us

profile of v1, /device:TPU:6, one launch (start us, length us, event | category | flops | bytes accessed | tf_op | source)
XLA Modules:
  0.0 154.4 jit_solution(1983656510550289971)
XLA Ops:
  0.0 0.7 convert_bitcast_fusion
  0.7 1.3 pad_maximum_fusion.meta_ref
  2.0 150.9 %shard_map.73 = bf16[128,512]{1,0:T(8,128)(2,1)} custom-call(bf16[128,512]{1,0:T(8,128)(2,1)} %tok_ref.1, f32[16,128]{1,0:T(8,128)} %pad_maximum_fusion.meta_ref, bf16[1,2,512,1024]{3,2,1,0:T(8,128)(2,1)} %gate_ref.1, bf16[1,1024,512]{2,1,0:T(8,128)(2,1)} %down_ref.1, bf16[1,2,512,512]{3,2,1,0:T(8,128)(2,1)} %sup_ref.1, bf16[1,1024,256]{2,1,0:T(8,128)(2,1)} %sdown_ref.1), custom_call_target="tpu_custom_call" | custom-call | flops 5000000000 | bytes 6000000 | tf_op jit(solution)/shard_map/pallas_call | solution.py:456
  152.8 1.6 %copy.9 = bf16[128,512]{1,0:T(8,128)(2,1)} copy(bf16[128,512]{1,0:T(8,128)(2,1)} %shard_map.73) | data formatting | bytes 262144

commit v2 on v1

v2 whole, which is shorter than its diff:
```python
import jax
import jax.numpy as jnp
from jax import lax
from jax.experimental import pallas as pl
from jax.experimental.pallas import tpu as pltpu
from jax.sharding import PartitionSpec as P

NX, NY, NZ = 4, 4, 16
CAP = 16
BF = jnp.bfloat16
F32 = jnp.float32
MESH = pl.DeviceIdType.MESH
UNITS = NZ // 2
STEPS = UNITS + 10
DEEP = 4
PIECES = 8
PIECE = 128 // PIECES


def mod(value, n):
    return lax.rem(value, n)


def kernel(
    tok_ref, slot_ref, weight_ref, gate_ref, down_ref, sup_ref, sdown_ref, out_ref,
    wall, wd, wsd, tok_all, meta_all, sel, arr, part, crecv, qbuf, rhalf, rfull, hid, hother, outs,
    back, dense, zsend, zland,
    w_sem, z_s, z_r, m_s, m_r, y_s, y_r, c_s, c_r, xa_s, xa_r, xb_s, xb_r,
    g_s, g_r, h_s, h_r, ch_s, ch_r, o_s, o_r, zz_s, zz_r,
):
    dp = lax.axis_index("dp")
    ex = lax.axis_index("expert")
    x, c = dp // 2, mod(dp, 2)
    y, z = ex // NZ, mod(ex, NZ)
    half = mod(z, 2)
    pair = z // 2
    x1, x2, x3 = mod(x + 1, NX), mod(x + 2, NX), mod(x + 3, NX)
    y1, y2, y3 = mod(y + 1, NY), mod(y + 2, NY), mod(y + 3, NY)
    z1, z3 = mod(z + 1, NZ), mod(z + NZ - 1, NZ)
    dev_xp, dev_xm = (x1 * 2 + c, ex), (x3 * 2 + c, ex)
    dev_c = (x * 2 + (1 - c), ex)
    dev_zp, dev_zm = (dp, y * NZ + z1), (dp, y * NZ + z3)
    mate = y * NZ + pair * 2 + (1 - half)
    dev_pt, dev_ptc = (dp, mate), (x * 2 + (1 - c), mate)
    dev_y = [(dp, row * NZ + z) for row in (y1, y2, y3)]

    def rc(src, dst, ssem, rsem, dev):
        return pltpu.make_async_remote_copy(
            src_ref=src, dst_ref=dst, send_sem=ssem, recv_sem=rsem, device_id=dev, device_id_type=MESH
        )

    loads = [
        pltpu.make_async_copy(gate_ref.at[0, 0], wall.at[:, 0:1024], w_sem.at[0]),
        pltpu.make_async_copy(gate_ref.at[0, 1], wall.at[:, 1024:2048], w_sem.at[1]),
        pltpu.make_async_copy(sup_ref.at[0, 0], wall.at[:, 2048:2560], w_sem.at[2]),
        pltpu.make_async_copy(sup_ref.at[0, 1], wall.at[:, 2560:3072], w_sem.at[3]),
        pltpu.make_async_copy(down_ref.at[0], wd, w_sem.at[4]),
        pltpu.make_async_copy(sdown_ref.at[0], wsd, w_sem.at[5]),
    ]
    for load in loads:
        load.start()

    tok_all[z] = tok_ref[...]
    meta_all[z, 0:8] = slot_ref[...].astype(F32)
    meta_all[z, 8:16] = weight_ref[...]

    barrier = pltpu.get_barrier_semaphore()
    for dev in (dev_xp, dev_xm, dev_c, dev_zp, dev_zm, dev_ptc, *dev_y):
        pl.semaphore_signal(barrier, inc=1, device_id=dev, device_id_type=MESH)
    pl.semaphore_wait(barrier, 9)

    def z_block(d, i):
        return mod(z + NZ - i, NZ) if d == 0 else mod(z + i, NZ)

    def z_copy(d, i, k, block):
        piece = tok_all.at[block, PIECE * k:PIECE * k + PIECE]
        at = (d, mod(i, 2), k)
        return rc(piece, piece, z_s.at[at], z_r.at[at], dev_zp if d == 0 else dev_zm)

    def m_copy(d, i, block):
        piece = meta_all.at[block]
        at = (d, mod(i, 2))
        return rc(piece, piece, m_s.at[at], m_r.at[at], dev_zp if d == 0 else dev_zm)

    def hop_send(d, i, k):
        z_copy(d, i, k, z_block(d, i)).start()

    def hop_left(d, i, k):
        z_copy(d, i, k, z_block(d, i)).wait_send()

    def hop_wait(d, i, k):
        z_copy(d, i, k, z_block(d, i + 1)).wait_recv()

    group = lax.broadcasted_iota(jnp.int32, (8, 128), 0)
    tri = (
        lax.broadcasted_iota(jnp.int32, (128, 128), 0) < lax.broadcasted_iota(jnp.int32, (128, 128), 1)
    ).astype(BF)
    place = lax.broadcasted_iota(jnp.int32, (8, CAP, 128), 1).astype(F32)

    def slot_ids(row, spare):
        own = row * NZ + z
        return jnp.where(spare == 1, NY * NZ + own // 2, own).astype(F32)

    send_ids = slot_ids(mod(y + group // 2 + 1, NY), mod(group, 2))
    back_ids = slot_ids(mod(group, 4), group // 4)

    def codes(meta, ids):
        mask = jnp.zeros((8, 128), F32)
        for k in range(8):
            mask = mask + jnp.where(meta[k:k + 1, :] == ids, 1.0, 0.0)
        rank = jnp.dot(mask.astype(BF), tri, preferred_element_type=F32)
        code = jnp.where(mask > 0.5, rank, -1.0)
        return jnp.broadcast_to(code[:, None, :], (8, CAP, 128)) == place

    def y_copy(d, h, block, n):
        at = (d, mod(h, DEEP), n)
        return rc(sel.at[block, 32 * n:32 * n + 32], arr.at[block, y], y_s.at[at], y_r.at[at], dev_y[n])

    def select_one(d, h):
        block = z_block(d, h)

        @pl.when(h >= DEEP + d)
        def _():
            for n in range(3):
                y_copy(d, h - DEEP, z_block(d, h - DEEP), n).wait_send()

        hot = codes(meta_all[block], send_ids)
        pick = jnp.where(hot, 1.0, 0.0).astype(BF).reshape(128, 128)
        rows = jnp.dot(pick, tok_all[block], preferred_element_type=F32).astype(BF)
        sel[block] = rows
        for n in range(3):
            y_copy(d, h, block, n).start()
        arr[block, y] = rows[96:128]

    def select(h):
        select_one(0, h)

        @pl.when((h >= 1) & (h <= 7))
        def _():
            select_one(1, h)

    def arrive(h):
        for n in range(3):
            y_copy(0, h, z_block(0, h), n).wait_recv()

        @pl.when((h >= 1) & (h <= 7))
        def _():
            for n in range(3):
                y_copy(1, h, z_block(1, h), n).wait_recv()

    def unit_of(u):
        near = jnp.where(u == 0, 0, jnp.where(u == 1, 1, jnp.where(u == 2, UNITS - 1, 2)))
        far = jnp.where(u == 4, 3, jnp.where(u == 5, 4, jnp.where(u == 6, UNITS - 3, UNITS - 2)))
        return mod(pair + jnp.where(u < 4, near, far), UNITS)

    def go(copy, u, n):
        @pl.when(u >= DEEP)
        def _():
            copy(u - DEEP, n).wait_send()

        copy(u, n).start()

    def c_copy(u, n):
        at = mod(u, DEEP)
        return rc(part.at[u, 1 - c], crecv.at[u], c_s.at[at], c_r.at[at], dev_c)

    def xa_copy(u, n):
        at = (mod(u, DEEP), n)
        cols = slice(1536 * n, 1536 * n + 1536)
        return rc(
            qbuf.at[u, x2, :, cols], rhalf.at[u, n], xa_s.at[at], xa_r.at[at], dev_xp if n == 0 else dev_xm
        )

    def xb_copy(u, n):
        at = (mod(u, DEEP), n)
        return rc(
            qbuf.at[u, x1 if n == 0 else x3], rfull.at[u, n], xb_s.at[at], xb_r.at[at],
            dev_xp if n == 0 else dev_xm,
        )

    def g_copy(u, n):
        at = (mod(u, DEEP), n)
        piece = hid.at[u, c, x]
        return rc(piece, piece, g_s.at[at], g_r.at[at], dev_xp if n == 0 else dev_xm)

    def h_copy(u, n):
        at = (mod(u, DEEP), n)
        piece = hid.at[u, c, x3 if n == 0 else x1, :, 768 * n:768 * n + 768]
        return rc(piece, piece, h_s.at[at], h_r.at[at], dev_xp if n == 0 else dev_xm)

    def ch_copy(u, n, rows):
        at = (mod(u, DEEP), n)
        if n == 0:
            piece = hid.at[u, c, rows]
            return rc(piece, piece, ch_s.at[at], ch_r.at[at], dev_c)
        return rc(
            hid.at[u, c, rows, :, 1024:1536], hother.at[u, c, rows], ch_s.at[at], ch_r.at[at],
            dev_pt if n == 1 else dev_ptc,
        )

    def ch_send(u, row):
        for n in (1, 2, 0):
            ch_copy(u, n, row).start()

    def o_copy(u, n):
        at = (mod(u, DEEP), n)
        return rc(outs.at[u, (y1, y2, y3)[n]], back.at[u, y], o_s.at[at], o_r.at[at], dev_y[n])

    def multiply_up(u):
        @pl.when(u == 0)
        def _():
            for load in loads[:4]:
                load.wait()

        q = unit_of(u)
        own = arr[pl.ds(2 * q, 2), :, 0:16, :].reshape(128, 512)
        spare = arr[pl.ds(2 * q, 2), :, 16:32, :].reshape(128, 512)
        for n in range(6):
            cols = slice(512 * n, 512 * n + 512)
            made = jnp.dot(own if n < 4 else spare, wall[:, cols], preferred_element_type=F32)
            part[u, :, :, :, cols] = made.astype(BF).reshape(2, 4, 16, 512)
        go(c_copy, u, 0)

    def add_core(u):
        c_copy(u, 0).wait_recv()
        for n, row in enumerate((x2, x1, x3, x)):
            qbuf[u, row] = (part[u, c, row].astype(F32) + crecv[u, row].astype(F32)).astype(BF)
            if n == 0:
                go(xa_copy, u, 0)
                go(xa_copy, u, 1)

    def add_far(u):
        for n, row, cols in ((0, x1, slice(0, 1536)), (1, x3, slice(1536, 3072))):
            xa_copy(u, n).wait_recv()
            both = qbuf[u, row, :, cols].astype(F32) + rhalf[u, n].astype(F32)
            qbuf[u, row, :, cols] = both.astype(BF)
            go(xb_copy, u, n)

    def activate(u):
        xb_copy(u, 0).wait_recv()
        xb_copy(u, 1).wait_recv()

        def total(low, width):
            cols = slice(low, low + width)
            mine = qbuf[u, x, :, cols].astype(F32)
            return mine + rfull[u, 0, :, cols].astype(F32) + rfull[u, 1, :, cols].astype(F32)

        def silu_product(low, width):
            gate = total(low, width)
            return (gate / (1.0 + jnp.exp(-gate)) * total(low + width, width)).astype(BF)

        hid[u, c, x, :, 1024:1536] = silu_product(2048, 512)
        hid[u, c, x, :, 0:1024] = silu_product(0, 1024)
        for n in (0, 1):
            go(g_copy, u, n)

        @pl.when(u >= DEEP)
        def _():
            for n in range(3):
                ch_copy(u - DEEP, n, slice(0, 4)).wait_send()

        ch_send(u, x)

    def gather_far(u):
        for n in (0, 1):
            g_copy(u, n).wait_recv()
            go(h_copy, u, n)
        ch_send(u, x3)
        ch_send(u, x1)

    def gather_core(u):
        h_copy(u, 0).wait_recv()
        h_copy(u, 1).wait_recv()
        ch_send(u, x2)

    def multiply_down(u):
        @pl.when(u == 0)
        def _():
            for load in loads[4:]:
                load.wait()

        for n in range(3):
            ch_copy(u, n, slice(0, 4)).wait_recv()
        own = hid[u, :, :, :, 0:1024].reshape(128, 1024)
        mine = hid[u, :, :, :, 1024:1536].reshape(128, 512)
        other = hother[u].reshape(128, 512)
        low = wsd[pl.ds(pl.multiple_of(half * 512, 512), 512), :]
        high = wsd[pl.ds(pl.multiple_of((1 - half) * 512, 512), 512), :]
        spare_sum = jnp.dot(mine, low, preferred_element_type=F32)
        spare_sum = spare_sum + jnp.dot(other, high, preferred_element_type=F32)
        own_out = jnp.dot(own, wd[...], preferred_element_type=F32).astype(BF).reshape(2, 4, 16, 512)
        spare_out = spare_sum.astype(BF).reshape(2, 4, 16, 256)
        for p in (0, 1):
            outs[u, :, p, :, 0:512] = own_out[p]
            outs[u, :, p, :, 512:768] = spare_out[p]
        for n in range(3):
            go(o_copy, u, n)
        back[u, y] = outs[u, y]

    def combine(u):
        for n in range(3):
            o_copy(u, n).wait_recv()
        q = unit_of(u)
        at = pl.ds(pl.multiple_of(half * 256, 256), 256)
        for p in (0, 1):
            block = 2 * q + p
            meta = meta_all[block]
            share = jnp.zeros((8, 128), F32)
            for k in range(8):
                share = share + jnp.where(meta[k:k + 1, :] == back_ids, meta[8 + k:9 + k, :], 0.0)
            spread = jnp.broadcast_to(share[:, None, :], (8, CAP, 128))
            weight = jnp.where(codes(meta, back_ids), spread, 0.0).astype(BF).reshape(128, 128)
            own = back[u, :, p, :, 0:512].reshape(64, 512)
            spare = back[u, :, p, :, 512:768].reshape(64, 256)
            over = (((0,), (0,)), ((), ()))
            dense[block] = lax.dot_general(weight[0:64], own, over, preferred_element_type=F32)
            more = lax.dot_general(weight[64:128], spare, over, preferred_element_type=F32)
            dense[block, :, at] = dense[block, :, at] + more

    def hops(h):
        @pl.when(h == 0)
        def _():
            for d in (0, 1):
                m_copy(d, 0, z_block(d, 0)).start()
            for k in range(PIECES):
                for d in (0, 1):
                    hop_send(d, 0, k)

        @pl.when((h >= 1) & (h <= 7))
        def _():
            for d in (0, 1):
                m_copy(d, h - 1, z_block(d, h)).wait_recv()

            @pl.when(h >= 2)
            def _():
                for d in (0, 1):
                    m_copy(d, h - 2, z_block(d, h - 2)).wait_send()

            m_copy(0, h, z_block(0, h)).start()

            @pl.when(h <= 6)
            def _():
                m_copy(1, h, z_block(1, h)).start()

            for k in range(PIECES):
                for d in (0, 1):
                    hop_wait(d, h - 1, k)

                @pl.when(h >= 2)
                def _():
                    for d in (0, 1):
                        hop_left(d, h - 2, k)

                hop_send(k // (PIECES // 2), h, k)

                @pl.when(h <= 6)
                def _():
                    hop_send(1 - k // (PIECES // 2), h, k)

        @pl.when(h == 8)
        def _():
            m_copy(0, 7, z_block(0, 8)).wait_recv()
            for k in range(PIECES):
                hop_wait(k // (PIECES // 2), 7, k)

    def take(h):
        hops(h)

        @pl.when(h >= 2)
        def _():
            arrive(h - 2)

        select(h)

    def zz_copy(d, j, k):
        rows = slice(PIECE * k, PIECE * k + PIECE)
        at = (d, mod(j, 2), k)
        return rc(
            zsend.at[d, j, rows], zland.at[d, j, rows], zz_s.at[at], zz_r.at[at],
            dev_zm if d == 0 else dev_zp,
        )

    def chain(j, first, second):
        for k in range(PIECES):
            rows = slice(PIECE * k, PIECE * k + PIECE)
            if not first:
                for d in (0, 1):
                    if not (second and k // (PIECES // 2) != d):
                        zz_copy(d, j - 1, k).wait_recv()
            for d in (0, 1):
                if first and k // (PIECES // 2) != d:
                    continue
                block = mod(z + NZ - 8 + j, NZ) if d == 0 else mod(z + 8 - j, NZ)
                value = dense[block, rows]
                if not first and not (second and k // (PIECES // 2) != d):
                    value = value + zland[d, j - 1, rows].astype(F32)
                zsend[d, j, rows] = value.astype(BF)
                if not first and not second:
                    @pl.when((j >= 3) | (k // (PIECES // 2) == d))
                    def _():
                        zz_copy(d, j - 2, k).wait_send()
                zz_copy(d, j, k).start()

    stages = [
        (0, multiply_up), (4, gather_core), (3, gather_far), (1, add_far), (2, activate), (0, add_core),
        (4, multiply_down),
    ]
    late = [(5, combine)]

    def run(t, which):
        for offset, stage in which:
            e = t - offset
            near = (e == 3) | ((e >= 5) & (e <= 7))

            @pl.when(near | ((e >= 9) & (e <= 12)))
            def _():
                stage(jnp.where(e == 3, 0, jnp.where(e <= 7, e - 4, e - 5)))

    def step(t, carry):
        @pl.when(t <= 8)
        def _():
            take(t)

        @pl.when((t == 9) | (t == 10))
        def _():
            arrive(t - 2)

        @pl.when(t == STEPS - 1)
        def _():
            chain(2, False, False)

        run(t, stages)

        run(t, late)

        @pl.when(t == STEPS - 3)
        def _():
            chain(0, True, False)

        @pl.when(t == STEPS - 2)
        def _():
            chain(1, False, True)

        return carry

    lax.fori_loop(0, STEPS, step, 0)

    def chain_step(j, carry):
        chain(j, False, False)
        return carry

    lax.fori_loop(3, 8, chain_step, 0)
    for k in range(PIECES):
        rows = slice(PIECE * k, PIECE * k + PIECE)
        for d in (0, 1):
            zz_copy(d, 7, k).wait_recv()
        value = dense[z, rows] + zland[0, 7, rows].astype(F32) + zland[1, 7, rows].astype(F32)
        out_ref[rows] = value.astype(BF)

    for d, i in ((0, 6), (1, 6), (0, 7)):
        m_copy(d, i, z_block(d, i)).wait_send()
    for k in range(PIECES):
        for d in (0, 1):
            hop_left(d, 6, k)
            zz_copy(d, 6, k).wait_send()
            zz_copy(d, 7, k).wait_send()
        hop_left(k // (PIECES // 2), 7, k)
    for n in range(3):
        for i in range(4):
            y_copy(0, 5 + i, z_block(0, 5 + i), n).wait_send()
            y_copy(1, 4 + i, z_block(1, 4 + i), n).wait_send()
    for u in range(UNITS - DEEP, UNITS):
        c_copy(u, 0).wait_send()
        for n in range(3):
            ch_copy(u, n, slice(0, 4)).wait_send()
            o_copy(u, n).wait_send()
        for copy in (xa_copy, xb_copy, g_copy, h_copy):
            for n in range(2):
                copy(u, n).wait_send()


def on_device(tokens, slot_of, weight_of, gate_up, down_proj, spare_up, spare_down):
    vmem = pl.BlockSpec(memory_space=pltpu.VMEM)
    hbm = pl.BlockSpec(memory_space=pl.ANY)
    dma = pltpu.SemaphoreType.DMA
    return pl.pallas_call(
        kernel,
        out_shape=jax.ShapeDtypeStruct((128, 512), BF),
        in_specs=[vmem, vmem, vmem, hbm, hbm, hbm, hbm],
        out_specs=vmem,
        scratch_shapes=[
            pltpu.VMEM((512, 3072), BF),
            pltpu.VMEM((1024, 512), BF),
            pltpu.VMEM((1024, 256), BF),
            pltpu.VMEM((NZ, 128, 512), BF),
            pltpu.VMEM((NZ, 16, 128), F32),
            pltpu.VMEM((NZ, 128, 512), BF),
            pltpu.VMEM((NZ, NY, 32, 512), BF),
            pltpu.VMEM((UNITS, 2, 4, 16, 3072), BF),
            pltpu.VMEM((UNITS, 4, 16, 3072), BF),
            pltpu.VMEM((UNITS, 4, 16, 3072), BF),
            pltpu.VMEM((UNITS, 2, 16, 1536), BF),
            pltpu.VMEM((UNITS, 2, 16, 3072), BF),
            pltpu.VMEM((UNITS, 2, 4, 16, 1536), BF),
            pltpu.VMEM((UNITS, 2, 4, 16, 512), BF),
            pltpu.VMEM((UNITS, 4, 2, 16, 768), BF),
            pltpu.VMEM((UNITS, 4, 2, 16, 768), BF),
            pltpu.VMEM((NZ, 128, 512), F32),
            pltpu.VMEM((2, 8, 128, 512), BF),
            pltpu.VMEM((2, 8, 128, 512), BF),
            dma((6,)),
            dma((2, 2, PIECES)), dma((2, 2, PIECES)),
            dma((2, 2)), dma((2, 2)),
            dma((2, 4, 3)), dma((2, 4, 3)),
            dma((4,)), dma((4,)),
            dma((4, 2)), dma((4, 2)),
            dma((4, 2)), dma((4, 2)),
            dma((4, 2)), dma((4, 2)),
            dma((4, 2)), dma((4, 2)),
            dma((4, 3)), dma((4, 3)),
            dma((4, 3)), dma((4, 3)),
            dma((2, 2, PIECES)), dma((2, 2, PIECES)),
        ],
        compiler_params=pltpu.CompilerParams(
            collective_id=0, has_side_effects=True, vmem_limit_bytes=58 * 1024 * 1024
        ),
        cost_estimate=pl.CostEstimate(flops=5 * 10**9, bytes_accessed=6 * 10**6, transcendentals=10**5),
    )(tokens, slot_of.T, weight_of.T, gate_up, down_proj, spare_up, spare_down)


def solution(mesh):
    in_specs = (
        P("expert", "dp"),
        P("expert", None),
        P("expert", None),
        P("expert", None, "dp", None),
        P("expert", None, "dp"),
        P("expert", None, "dp", None),
        P("expert", None, "dp"),
    )
    out_specs = P("expert", "dp")
    return jax.shard_map(
        on_device, mesh=mesh, in_specs=in_specs, out_specs=out_specs, check_vma=False
    )
```

time: 155 us -> 127 us (0.82)
  Pallas kernels: 151 us -> 124 us
  other arithmetic: 1.97 us -> 0 us
    pallas_call x1, Pallas kernels: 151 us -> 124 us  [on_device(): pl.pallas_call(kernel, out_shape=jax.ShapeDtypeStruct((128, 512), BF), in...]
where the time goes in v2:
time: 127 us; the launch traced here: 126 us
  Pallas kernels  124 us (98%)
  local copies, waits for them, and re-layouts  1.57 us (1%)
    pallas_call x1, Pallas kernels, on_device(): pl.pallas_call(kernel, out_shape=jax.ShapeDtypeStruct((128, 512), BF), in...  124 us

profile of v2, /device:TPU:6, one launch (start us, length us, event | category | flops | bytes accessed | tf_op | source)
XLA Modules:
  0.0 125.6 jit_solution(6333390460811418256)
XLA Ops:
  0.0 124.0 %shard_map.73 = bf16[128,512]{1,0:T(8,128)(2,1)} custom-call(bf16[128,512]{1,0:T(8,128)(2,1)} %tok_ref.1, s32[8,128]{1,0:T(8,128)} %bitcast.2, f32[8,128]{1,0:T(8,128)} %bitcast.3, bf16[1,2,512,1024]{3,2,1,0:T(8,128)(2,1)} %gate_ref.1, bf16[1,1024,512]{2,1,0:T(8,128)(2,1)} %down_ref.1, bf16[1,2,512,512]{3,2,1,0:T(8,128)(2,1)} %sup_ref.1, ...), custom_call_target="tpu_custom_call" | custom-call | flops 5000000000 | bytes 6000000 | tf_op jit(solution)/shard_map/pallas_call | solution.py:486
  124.0 1.6 %copy.9 = bf16[128,512]{1,0:T(8,128)(2,1)} copy(bf16[128,512]{1,0:T(8,128)(2,1)} %shard_map.73) | data formatting | bytes 262144

commit v3 on v2

v3 whole, which is shorter than its diff:
```python
import jax
import jax.numpy as jnp
from jax import lax
from jax.experimental import pallas as pl
from jax.experimental.pallas import tpu as pltpu
from jax.sharding import PartitionSpec as P

NX, NY, NZ = 4, 4, 16
CAP = 16
BF = jnp.bfloat16
F32 = jnp.float32
MESH = pl.DeviceIdType.MESH
UNITS = NZ // 2
PARTS = 3 * UNITS
STEPS = PARTS + 19
DEEP = 4
MANY = 8
PIECES = 8
PIECE = 128 // PIECES


def mod(value, n):
    return lax.rem(value, n)


def kernel(
    tok_ref, slot_ref, weight_ref, gate_ref, down_ref, sup_ref, sdown_ref, out_ref,
    wall, wd, wsd, tok_all, meta_all, sel, arr, part, crecv, qbuf, rhalf, rfull, hid, hother, outs,
    back, dense, zsend, zland,
    w_sem, sent, z_r, m_r, y_r, c_r, xa_r, xb_r, g_r, h_r, ch_r, pt_r, o_r, zz_r,
):
    dp = lax.axis_index("dp")
    ex = lax.axis_index("expert")
    x, c = dp // 2, mod(dp, 2)
    y, z = ex // NZ, mod(ex, NZ)
    half = mod(z, 2)
    pair = z // 2
    x1, x2, x3 = mod(x + 1, NX), mod(x + 2, NX), mod(x + 3, NX)
    y1, y2, y3 = mod(y + 1, NY), mod(y + 2, NY), mod(y + 3, NY)
    z1, z3 = mod(z + 1, NZ), mod(z + NZ - 1, NZ)
    dev_xp, dev_xm = (x1 * 2 + c, ex), (x3 * 2 + c, ex)
    dev_c = (x * 2 + (1 - c), ex)
    dev_zp, dev_zm = (dp, y * NZ + z1), (dp, y * NZ + z3)
    mate = y * NZ + pair * 2 + (1 - half)
    dev_pt, dev_ptc = (dp, mate), (x * 2 + (1 - c), mate)
    dev_y = [(dp, row * NZ + z) for row in (y1, y2, y3)]

    def rc(src, dst, kind, rsem, dev):
        return pltpu.make_async_remote_copy(
            src_ref=src, dst_ref=dst, send_sem=sent.at[kind], recv_sem=rsem, device_id=dev, device_id_type=MESH
        )

    def await_all(ref, rsem):
        rc(ref, ref, 0, rsem, dev_c).wait_recv()

    pairs = (
        (sup_ref, 0, slice(0, 512)), (gate_ref, 1, slice(0, 512)), (gate_ref, 2, slice(512, 1024)),
    )
    loads = []
    for ref, n, cols in pairs:
        for g in (0, 1):
            into = wall.at[n, :, 512 * g:512 * g + 512]
            loads.append(pltpu.make_async_copy(ref.at[0, g, :, cols], into, w_sem.at[len(loads)]))
    loads.append(pltpu.make_async_copy(down_ref.at[0], wd, w_sem.at[6]))
    loads.append(pltpu.make_async_copy(sdown_ref.at[0], wsd, w_sem.at[7]))
    for load in loads:
        load.start()

    tok_all[z] = tok_ref[...]
    meta_all[z, 0:8] = slot_ref[...].astype(F32)
    meta_all[z, 8:16] = weight_ref[...]

    barrier = pltpu.get_barrier_semaphore()
    for dev in (dev_xp, dev_xm, dev_c, dev_zp, dev_zm, dev_ptc, *dev_y):
        pl.semaphore_signal(barrier, inc=1, device_id=dev, device_id_type=MESH)
    pl.semaphore_wait(barrier, 9)

    def z_block(d, i):
        return mod(z + NZ - i, NZ) if d == 0 else mod(z + i, NZ)

    def z_copy(d, i, k, block):
        piece = tok_all.at[block, PIECE * k:PIECE * k + PIECE]
        return rc(piece, piece, 0, z_r.at[mod(i, 2), k], dev_zp if d == 0 else dev_zm)

    def m_copy(d, i, block):
        piece = meta_all.at[block]
        return rc(piece, piece, 1, m_r.at[mod(i, 2)], dev_zp if d == 0 else dev_zm)

    def hop_send(d, i, k):
        z_copy(d, i, k, z_block(d, i)).start()

    def hop_wait(i, k, rows):
        await_all(tok_all.at[0, 0:rows], z_r.at[mod(i, 2), k])

    group = lax.broadcasted_iota(jnp.int32, (8, 128), 0)
    tri = (
        lax.broadcasted_iota(jnp.int32, (128, 128), 0) < lax.broadcasted_iota(jnp.int32, (128, 128), 1)
    ).astype(BF)
    place = lax.broadcasted_iota(jnp.int32, (8, CAP, 128), 1).astype(F32)

    def slot_ids(row, spare):
        own = row * NZ + z
        return jnp.where(spare == 1, NY * NZ + own // 2, own).astype(F32)

    send_ids = slot_ids(mod(y + group // 2 + 1, NY), mod(group, 2))
    back_ids = slot_ids(mod(group, 4), group // 4)

    def codes(meta, ids):
        mask = jnp.zeros((8, 128), F32)
        for k in range(8):
            mask = mask + jnp.where(meta[k:k + 1, :] == ids, 1.0, 0.0)
        rank = jnp.dot(mask.astype(BF), tri, preferred_element_type=F32)
        code = jnp.where(mask > 0.5, rank, -1.0)
        return jnp.broadcast_to(code[:, None, :], (8, CAP, 128)) == place

    def y_copy(d, h, block, n):
        at = (d, mod(h, DEEP))
        return rc(sel.at[block, 2 * n:2 * n + 2], arr.at[block, y], 2, y_r.at[at], dev_y[n])

    def select_one(d, h):
        block = z_block(d, h)

        hot = codes(meta_all[block], send_ids)
        pick = jnp.where(hot, 1.0, 0.0).astype(BF).reshape(128, 128)
        rows = jnp.dot(pick, tok_all[block], preferred_element_type=F32).astype(BF)
        sel[block] = rows.reshape(8, CAP, 512)
        for n in range(3):
            y_copy(d, h, block, n).start()
        arr[block, y] = rows[96:128].reshape(2, CAP, 512)

    def select(h):
        select_one(0, h)

        @pl.when((h >= 1) & (h <= 7))
        def _():
            select_one(1, h)

    def arrive(h):
        await_all(sel.at[0, 0:6], y_r.at[0, mod(h, DEEP)])

        @pl.when((h >= 1) & (h <= 7))
        def _():
            await_all(sel.at[0, 0:6], y_r.at[1, mod(h, DEEP)])

    def unit_of(u):
        shift = jnp.int32(0)
        for n, at in enumerate((0, 1, -1, 2, -3, 4, 3, -2)):
            shift = jnp.where(u == n, at, shift)
        return 2 * mod(pair + shift + UNITS, UNITS), 2 * mod(pair - shift + UNITS, UNITS) + 1

    def go(copy, u, n):
        copy(u, n).start()

    def c_copy(w):
        return rc(part.at[w, 1 - c], crecv.at[w], 3, c_r.at[mod(w, MANY)], dev_c)

    def near(n):
        return dev_xp if n == 0 else dev_xm

    def xa_copy(w, n):
        cols = slice(512 * n, 512 * n + 512)
        return rc(qbuf.at[w, x2, :, cols], rhalf.at[w, n], 4, xa_r.at[mod(w, MANY)], near(n))

    def xb_copy(w, n):
        cols = slice(512 * n, 512 * n + 512)
        row = x1 if n == 0 else x3
        return rc(qbuf.at[w, row, :, cols], rfull.at[w, n, :, cols], 5, xb_r.at[mod(w, MANY)], near(n))

    def xd_copy(w, n):
        cols = slice(512 * (1 - n), 512 * (1 - n) + 512)
        row = x1 if n == 0 else x3
        return rc(qbuf.at[w, row, :, cols], rfull.at[w, n, :, cols], 5, xb_r.at[mod(w, MANY)], near(n))

    def g_copy(w, n):
        piece = hid.at[w, c, x]
        return rc(piece, piece, 6, g_r.at[mod(w, MANY)], near(n))

    def h_copy(w, n):
        piece = hid.at[w, c, x3 if n == 0 else x1, :, 256 * n:256 * n + 256]
        return rc(piece, piece, 7, h_r.at[mod(w, MANY)], near(n))

    def ch_copy(w):
        piece = hid.at[w, c]
        return rc(piece, piece, 8, ch_r.at[mod(w // 3, DEEP)], dev_c)

    def pt_copy(u, n):
        return rc(
            hid.at[3 * u, c], hother.at[u, c], 11, pt_r.at[mod(u, DEEP)], dev_pt if n == 0 else dev_ptc
        )

    def ch_send(w):
        @pl.when(mod(w, 3) == 0)
        def _():
            for n in (0, 1):
                pt_copy(w // 3, n).start()

        ch_copy(w).start()

    def o_copy(u, n):
        return rc(outs.at[u, (y1, y2, y3)[n]], back.at[u, y], 9, o_r.at[mod(u, DEEP)], dev_y[n])

    def multiply_up(w):
        u, n = w // 3, mod(w, 3)
        for i in range(3):
            @pl.when(w == i)
            def _():
                loads[2 * i].wait()
                loads[2 * i + 1].wait()

        which = jnp.where(n == 0, 1, 0)
        rows = jnp.concatenate([arr[block, :, which].reshape(64, 512) for block in unit_of(u)], 0)
        for g in (0, 1):
            cols = slice(512 * g, 512 * g + 512)
            made = jnp.dot(rows, wall[n, :, cols], preferred_element_type=F32)
            part[w, :, :, :, cols] = made.astype(BF).reshape(2, 4, 16, 512)
        c_copy(w).start()

    def add_core(w):
        c_copy(w).wait_recv()
        for n, row in enumerate((x2, x1, x3, x)):
            qbuf[w, row] = (part[w, c, row].astype(F32) + crecv[w, row].astype(F32)).astype(BF)
            if n == 0:
                go(xa_copy, w, 0)
                go(xa_copy, w, 1)
            elif n <= 2:
                go(xd_copy, w, n - 1)

    def add_far(w):
        await_all(rhalf.at[w], xa_r.at[mod(w, MANY)])
        for n, row, cols in ((0, x1, slice(0, 512)), (1, x3, slice(512, 1024))):
            both = qbuf[w, row, :, cols].astype(F32) + rhalf[w, n].astype(F32)
            qbuf[w, row, :, cols] = both.astype(BF)
            go(xb_copy, w, n)

    def activate(w):
        await_all(rfull.at[w], xb_r.at[mod(w, MANY)])

        def total(low, width):
            cols = slice(low, low + width)
            mine = qbuf[w, x, :, cols].astype(F32)
            return mine + rfull[w, 0, :, cols].astype(F32) + rfull[w, 1, :, cols].astype(F32)

        gate = total(0, 512)
        hid[w, c, x] = (gate / (1.0 + jnp.exp(-gate)) * total(512, 512)).astype(BF)
        for n in (0, 1):
            go(g_copy, w, n)

    def gather_far(w):
        await_all(hid.at[w, c, 0:2], g_r.at[mod(w, MANY)])
        for n in (0, 1):
            go(h_copy, w, n)

    def gather_core(w):
        await_all(hid.at[w, c, 0], h_r.at[mod(w, MANY)])
        ch_send(w)

    def multiply_down(u):
        @pl.when(u == 0)
        def _():
            for load in loads[6:]:
                load.wait()

        await_all(hother.at[u], pt_r.at[mod(u, DEEP)])
        await_all(hid.at[0:3, 0], ch_r.at[mod(u, DEEP)])
        mine, first, second = [hid[3 * u + n].reshape(128, 512) for n in range(3)]
        other = hother[u].reshape(128, 512)
        low = wsd[pl.ds(pl.multiple_of(half * 512, 512), 512), :]
        high = wsd[pl.ds(pl.multiple_of((1 - half) * 512, 512), 512), :]
        spare_sum = jnp.dot(mine, low, preferred_element_type=F32)
        spare_sum = spare_sum + jnp.dot(other, high, preferred_element_type=F32)
        own_sum = jnp.dot(first, wd[0:512], preferred_element_type=F32)
        own_sum = own_sum + jnp.dot(second, wd[512:1024], preferred_element_type=F32)
        own_out = own_sum.astype(BF).reshape(2, 4, 16, 512)
        spare_out = spare_sum.astype(BF).reshape(2, 4, 16, 256)
        for p in (0, 1):
            outs[u, :, p, :, 0:512] = own_out[p]
            outs[u, :, p, :, 512:768] = spare_out[p]
        for n in range(3):
            go(o_copy, u, n)
        back[u, y] = outs[u, y]

    def combine(u):
        await_all(outs.at[u, 0:3], o_r.at[mod(u, DEEP)])
        at = pl.ds(pl.multiple_of(half * 256, 256), 256)
        for p, block in enumerate(unit_of(u)):
            meta = meta_all[block]
            share = jnp.zeros((8, 128), F32)
            for k in range(8):
                share = share + jnp.where(meta[k:k + 1, :] == back_ids, meta[8 + k:9 + k, :], 0.0)
            spread = jnp.broadcast_to(share[:, None, :], (8, CAP, 128))
            weight = jnp.where(codes(meta, back_ids), spread, 0.0).astype(BF).reshape(128, 128)
            own = back[u, :, p, :, 0:512].reshape(64, 512)
            spare = back[u, :, p, :, 512:768].reshape(64, 256)
            over = (((0,), (0,)), ((), ()))
            dense[block] = lax.dot_general(weight[0:64], own, over, preferred_element_type=F32)
            more = lax.dot_general(weight[64:128], spare, over, preferred_element_type=F32)
            dense[block, :, at] = dense[block, :, at] + more

    def hops(h):
        @pl.when(h == 0)
        def _():
            for d in (0, 1):
                m_copy(d, 0, z_block(d, 0)).start()
            for k in range(PIECES):
                for d in (0, 1):
                    hop_send(d, 0, k)

        @pl.when((h >= 1) & (h <= 7))
        def _():
            await_all(meta_all.at[0:2], m_r.at[mod(h - 1, 2)])
            m_copy(0, h, z_block(0, h)).start()

            @pl.when(h <= 6)
            def _():
                m_copy(1, h, z_block(1, h)).start()

            for k in range(PIECES):
                hop_wait(h - 1, k, 2 * PIECE)

                hop_send(k // (PIECES // 2), h, k)

                @pl.when(h <= 6)
                def _():
                    hop_send(1 - k // (PIECES // 2), h, k)

        @pl.when(h == 8)
        def _():
            await_all(meta_all.at[0], m_r.at[1])
            for k in range(PIECES):
                hop_wait(7, k, PIECE)

    def take(h):
        hops(h)

        @pl.when(h >= 2)
        def _():
            arrive(h - 2)

        select(h)

    def zz_copy(d, j, k):
        rows = slice(PIECE * k, PIECE * k + PIECE)
        return rc(
            zsend.at[d, j, rows], zland.at[d, j, rows], 10, zz_r.at[mod(j, 2), k],
            dev_zm if d == 0 else dev_zp,
        )

    def chain(j, first, second):
        for k in range(PIECES):
            rows = slice(PIECE * k, PIECE * k + PIECE)
            if not first:
                await_all(tok_all.at[0, 0:PIECE if second else 2 * PIECE], zz_r.at[mod(j - 1, 2), k])
            for d in (0, 1):
                if first and k // (PIECES // 2) != d:
                    continue
                block = mod(z + NZ - 8 + j, NZ) if d == 0 else mod(z + 8 - j, NZ)
                value = dense[block, rows]
                if not first and not (second and k // (PIECES // 2) != d):
                    value = value + zland[d, j - 1, rows].astype(F32)
                zsend[d, j, rows] = value.astype(BF)
                zz_copy(d, j, k).start()

    stages = [
        (0, multiply_up), (1, add_core), (3, add_far), (5, activate), (7, gather_far), (9, gather_core),
    ]
    whole_stages = [(10, multiply_down), (13, combine)]

    def entry(t, offset):
        w = t - offset - 6
        return (w >= 0) & (w < PARTS), w

    def step(t, carry):
        @pl.when((t <= 16) & (mod(t, 2) == 0))
        def _():
            take(t // 2)

        @pl.when((t == 18) | (t == 20))
        def _():
            arrive(t // 2 - 2)

        for offset, stage in stages:
            live, w = entry(t, offset)

            @pl.when(live)
            def _():
                stage(w)

        for offset, stage in whole_stages:
            live, w = entry(t, offset)

            @pl.when(live & (mod(w + 3, 3) == 2))
            def _():
                stage(w // 3)

        @pl.when(t == 36)
        def _():
            chain(0, True, False)

        @pl.when(t == 38)
        def _():
            chain(1, False, True)

        @pl.when((t == 40) | (t == 42))
        def _():
            chain(t // 2 - 18, False, False)

        return carry

    lax.fori_loop(0, STEPS, step, 0)

    def chain_step(j, carry):
        chain(j, False, False)
        return carry

    lax.fori_loop(4, 8, chain_step, 0)
    for k in range(PIECES):
        rows = slice(PIECE * k, PIECE * k + PIECE)
        await_all(tok_all.at[0, 0:2 * PIECE], zz_r.at[1, k])
        value = dense[z, rows] + zland[0, 7, rows].astype(F32) + zland[1, 7, rows].astype(F32)
        out_ref[rows] = value.astype(BF)

    whole = (
        tok_all.at[0:15], meta_all.at[0:15], sel.at[0:12], crecv, rhalf, rfull, hid.at[0:6], hid.at[0:3],
        hid.at[0:12], outs.at[0:6], tok_all.at[0:15], hother,
    )
    for kind, ref in enumerate(whole):
        rc(ref, ref, kind, w_sem.at[0], dev_c).wait_send()


def on_device(tokens, slot_of, weight_of, gate_up, down_proj, spare_up, spare_down):
    vmem = pl.BlockSpec(memory_space=pltpu.VMEM)
    hbm = pl.BlockSpec(memory_space=pl.ANY)
    dma = pltpu.SemaphoreType.DMA
    return pl.pallas_call(
        kernel,
        out_shape=jax.ShapeDtypeStruct((128, 512), BF),
        in_specs=[vmem, vmem, vmem, hbm, hbm, hbm, hbm],
        out_specs=vmem,
        scratch_shapes=[
            pltpu.VMEM((3, 512, 1024), BF),
            pltpu.VMEM((1024, 512), BF),
            pltpu.VMEM((1024, 256), BF),
            pltpu.VMEM((NZ, 128, 512), BF),
            pltpu.VMEM((NZ, 16, 128), F32),
            pltpu.VMEM((NZ, 8, CAP, 512), BF),
            pltpu.VMEM((NZ, NY, 2, CAP, 512), BF),
            pltpu.VMEM((PARTS, 2, 4, 16, 1024), BF),
            pltpu.VMEM((PARTS, 4, 16, 1024), BF),
            pltpu.VMEM((PARTS, 4, 16, 1024), BF),
            pltpu.VMEM((PARTS, 2, 16, 512), BF),
            pltpu.VMEM((PARTS, 2, 16, 1024), BF),
            pltpu.VMEM((PARTS, 2, 4, 16, 512), BF),
            pltpu.VMEM((UNITS, 2, 4, 16, 512), BF),
            pltpu.VMEM((UNITS, 4, 2, 16, 768), BF),
            pltpu.VMEM((UNITS, 4, 2, 16, 768), BF),
            pltpu.VMEM((NZ, 128, 512), F32),
            pltpu.VMEM((2, 8, 128, 512), BF),
            pltpu.VMEM((2, 8, 128, 512), BF),
            dma((8,)),
            dma((12,)),
            dma((2, PIECES)),
            dma((2,)),
            dma((2, DEEP)),
            dma((MANY,)), dma((MANY,)), dma((MANY,)),
            dma((MANY,)), dma((MANY,)),
            dma((DEEP,)),
            dma((DEEP,)),
            dma((DEEP,)),
            dma((2, PIECES)),
        ],
        compiler_params=pltpu.CompilerParams(
            collective_id=0, has_side_effects=True, vmem_limit_bytes=58 * 1024 * 1024
        ),
        cost_estimate=pl.CostEstimate(flops=5 * 10**9, bytes_accessed=6 * 10**6, transcendentals=10**5),
    )(tokens, slot_of.T, weight_of.T, gate_up, down_proj, spare_up, spare_down)


def solution(mesh):
    in_specs = (
        P("expert", "dp"),
        P("expert", None),
        P("expert", None),
        P("expert", None, "dp", None),
        P("expert", None, "dp"),
        P("expert", None, "dp", None),
        P("expert", None, "dp"),
    )
    out_specs = P("expert", "dp")
    return jax.shard_map(
        on_device, mesh=mesh, in_specs=in_specs, out_specs=out_specs, check_vma=False
    )
```

time: 127 us -> 116 us (0.913)
  Pallas kernels: 124 us -> 114 us
    pallas_call x1, Pallas kernels: 124 us -> 114 us  [on_device(): pl.pallas_call(kernel, out_shape=jax.ShapeDtypeStruct((128, 512), BF), in...]
where the time goes in v3:
time: 116 us
  Pallas kernels  114 us (98%)
  local copies, waits for them, and re-layouts  1.57 us (1%)
    pallas_call x1, Pallas kernels, on_device(): pl.pallas_call(kernel, out_shape=jax.ShapeDtypeStruct((128, 512), BF), in...  114 us

profile of v3, /device:TPU:6, one launch (start us, length us, event | category | flops | bytes accessed | tf_op | source)
XLA Modules:
  0.0 115.8 jit_solution(14541460689187662309)
XLA Ops:
  0.0 114.2 %shard_map.73 = bf16[128,512]{1,0:T(8,128)(2,1)} custom-call(bf16[128,512]{1,0:T(8,128)(2,1)} %tok_ref.1, s32[8,128]{1,0:T(8,128)} %bitcast.2, f32[8,128]{1,0:T(8,128)} %bitcast.3, bf16[1,2,512,1024]{3,2,1,0:T(8,128)(2,1)} %gate_ref.1, bf16[1,1024,512]{2,1,0:T(8,128)(2,1)} %down_ref.1, bf16[1,2,512,512]{3,2,1,0:T(8,128)(2,1)} %sup_ref.1, ...), custom_call_target="tpu_custom_call" | custom-call | flops 5000000000 | bytes 6000000 | tf_op jit(solution)/shard_map/pallas_call | solution.py:434
  114.3 1.6 %copy.9 = bf16[128,512]{1,0:T(8,128)(2,1)} copy(bf16[128,512]{1,0:T(8,128)(2,1)} %shard_map.73) | data formatting | bytes 262144

commit v4 on v3

--- a/solution.py
+++ b/solution.py
@@ -12,7 +12,7 @@
 MESH = pl.DeviceIdType.MESH
 UNITS = NZ // 2
 PARTS = 3 * UNITS
-STEPS = PARTS + 19
+STEPS = PARTS + 18
 DEEP = 4
 MANY = 8
 PIECES = 8
@@ -26,7 +26,7 @@
 def kernel(
     tok_ref, slot_ref, weight_ref, gate_ref, down_ref, sup_ref, sdown_ref, out_ref,
     wall, wd, wsd, tok_all, meta_all, sel, arr, part, crecv, qbuf, rhalf, rfull, hid, hother, outs,
-    back, dense, zsend, zland,
+    back, dense, zsend, zland, slots,
     w_sem, sent, z_r, m_r, y_r, c_r, xa_r, xb_r, g_r, h_r, ch_r, pt_r, o_r, zz_r,
 ):
     dp = lax.axis_index("dp")
@@ -63,16 +63,21 @@
             loads.append(pltpu.make_async_copy(ref.at[0, g, :, cols], into, w_sem.at[len(loads)]))
     loads.append(pltpu.make_async_copy(down_ref.at[0], wd, w_sem.at[6]))
     loads.append(pltpu.make_async_copy(sdown_ref.at[0], wsd, w_sem.at[7]))
-    for load in loads:
+    firsts = [
+        pltpu.make_async_copy(tok_ref, tok_all.at[z], w_sem.at[8]),
+        pltpu.make_async_copy(slot_ref, slots, w_sem.at[9]),
+        pltpu.make_async_copy(weight_ref, meta_all.at[z, 8:16], w_sem.at[10]),
+    ]
+    for load in firsts + loads:
         load.start()
 
-    tok_all[z] = tok_ref[...]
-    meta_all[z, 0:8] = slot_ref[...].astype(F32)
-    meta_all[z, 8:16] = weight_ref[...]
 
     barrier = pltpu.get_barrier_semaphore()
     for dev in (dev_xp, dev_xm, dev_c, dev_zp, dev_zm, dev_ptc, *dev_y):
         pl.semaphore_signal(barrier, inc=1, device_id=dev, device_id_type=MESH)
+    for load in firsts:
+        load.wait()
+    meta_all[z, 0:8] = slots[...].astype(F32)
     pl.semaphore_wait(barrier, 9)
 
     def z_block(d, i):
@@ -332,10 +337,6 @@
     def take(h):
         hops(h)
 
-        @pl.when(h >= 2)
-        def _():
-            arrive(h - 2)
-
         select(h)
 
     def zz_copy(d, j, k):
@@ -366,7 +367,7 @@
     whole_stages = [(10, multiply_down), (13, combine)]
 
     def entry(t, offset):
-        w = t - offset - 6
+        w = t - offset - 5
         return (w >= 0) & (w < PARTS), w
 
     def step(t, carry):
@@ -374,9 +375,9 @@
         def _():
             take(t // 2)
 
-        @pl.when((t == 18) | (t == 20))
-        def _():
-            arrive(t // 2 - 2)
+        @pl.when((t >= 3) & (t <= 19) & (mod(t, 2) == 1))
+        def _():
+            arrive(t // 2 - 1)
 
         for offset, stage in stages:
             live, w = entry(t, offset)
@@ -392,17 +393,17 @@
             def _():
                 stage(w // 3)
 
-        @pl.when(t == 36)
+        @pl.when(t == 35)
         def _():
             chain(0, True, False)
 
-        @pl.when(t == 38)
+        @pl.when(t == 37)
         def _():
             chain(1, False, True)
 
-        @pl.when((t == 40) | (t == 42))
-        def _():
-            chain(t // 2 - 18, False, False)
+        @pl.when((t == 39) | (t == 41))
+        def _():
+            chain(t // 2 - 17, False, False)
 
         return carry
 
@@ -434,7 +435,7 @@
     return pl.pallas_call(
         kernel,
         out_shape=jax.ShapeDtypeStruct((128, 512), BF),
-        in_specs=[vmem, vmem, vmem, hbm, hbm, hbm, hbm],
+        in_specs=[hbm, hbm, hbm, hbm, hbm, hbm, hbm],
         out_specs=vmem,
         scratch_shapes=[
             pltpu.VMEM((3, 512, 1024), BF),
@@ -456,7 +457,8 @@
             pltpu.VMEM((NZ, 128, 512), F32),
             pltpu.VMEM((2, 8, 128, 512), BF),
             pltpu.VMEM((2, 8, 128, 512), BF),
-            dma((8,)),
+            pltpu.VMEM((8, 128), jnp.int32),
+            dma((11,)),
             dma((12,)),
             dma((2, PIECES)),
             dma((2,)),

time: 116 us -> 114 us (0.983)
  Pallas kernels: 114 us -> 112 us
    pallas_call x1, Pallas kernels: 114 us -> 112 us  [on_device(): pl.pallas_call(kernel, out_shape=jax.ShapeDtypeStruct((128, 512), BF), in...]
where the time goes in v4:
time: 114 us
  Pallas kernels  112 us (98%)
  local copies, waits for them, and re-layouts  1.57 us (1%)
    pallas_call x1, Pallas kernels, on_device(): pl.pallas_call(kernel, out_shape=jax.ShapeDtypeStruct((128, 512), BF), in...  112 us

profile of v4, /device:TPU:6, one launch (start us, length us, event | category | flops | bytes accessed | tf_op | source)
XLA Modules:
  0.0 113.7 jit_solution(7555400750645434090)
XLA Ops:
  0.0 112.1 %shard_map.73 = bf16[128,512]{1,0:T(8,128)(2,1)} custom-call(bf16[128,512]{1,0:T(8,128)(2,1)} %tok_ref.1, s32[8,128]{1,0:T(8,128)} %bitcast.2, f32[8,128]{1,0:T(8,128)} %bitcast.3, bf16[1,2,512,1024]{3,2,1,0:T(8,128)(2,1)} %gate_ref.1, bf16[1,1024,512]{2,1,0:T(8,128)(2,1)} %down_ref.1, bf16[1,2,512,512]{3,2,1,0:T(8,128)(2,1)} %sup_ref.1, ...), custom_call_target="tpu_custom_call" | custom-call | flops 5000000000 | bytes 6000000 | tf_op jit(solution)/shard_map/pallas_call | solution.py:435
  112.1 1.6 %copy.9 = bf16[128,512]{1,0:T(8,128)(2,1)} copy(bf16[128,512]{1,0:T(8,128)(2,1)} %shard_map.73) | data formatting | bytes 262144
